TPU v7x, 32 devices: a whole 2x2x4 slice. The times are simulated.
32 devices in a mesh: runs: 2 (over x), tm: 8 (over z, y), hyd: 2 (over core).
Axes of the slice: x: 2, y: 2, z: 4, core: 2. Of those that a mesh axis runs over, the one named last changes fastest.
Arguments:
- record: bfloat16 [524160, 1024], P(('runs', 'tm'), 'hyd'), parts along dimension 0, may hold values from -6 to 6
- chips: int32 [4095], replicated, may hold values from -1 to 1, as said below
- steer_lags: int32 [1024, 256], P('hyd'), may hold values from 0 to 7
Outputs:
- power: float32 [128, 512, 256], P('runs', 'tm', 'hyd'), parts along dimension 0
There are 2 independent parts, one for each index of `runs`. A program takes and returns all parts, laid end to end along the dimension named above; an argument that names none is the same for every part. Nothing has to cross between parts.
Inputs may be any that keep to these rules, and one draw needn't show every extreme that they name: The chips are +1 or -1 and form one period of a maximal-length sequence of period 4095, starting at a drawn phase.
All inputs are finite; a program needn't handle non-finite values.
Results may differ from a plain program's by a relative error of at most 0.0047.
Values may be sent and summed in bfloat16 or wider, within the bound.
A program may use at most 256 MiB of HBM per device.

v0:
```python
import math
import jax
import jax.numpy as jnp
from jax import lax
from jax.sharding import PartitionSpec as P

CODE = 4095
HYDRO = 1024
DELAYS = 512
PERIODS = 64
BEAMS = 256
MAXLAG = 8


def passed_along(array, axis, by):
    length = lax.axis_size(axis)
    pairs = [(i, i + by) for i in range(length) if 0 <= i + by < length]
    return lax.ppermute(array, axis, pairs)


def toeplitz_code(chips):
    seg_len = CODE + DELAYS - 1
    padded = jnp.concatenate([chips.astype(jnp.float32), jnp.zeros((DELAYS,), jnp.float32)])
    tiled = jnp.tile(padded, DELAYS)[: DELAYS * seg_len]
    return tiled.reshape(DELAYS, seg_len).astype(jnp.bfloat16)


def dft_table(length):
    freq = jnp.arange(length, dtype=jnp.int32)
    phase = (freq[:, None] * freq[None, :] % length).astype(jnp.float32) * (2.0 * math.pi / length)
    weight = 1.0 / math.sqrt(length)
    return jnp.concatenate([jnp.cos(phase) * weight, -jnp.sin(phase) * weight], 0).astype(
        jnp.bfloat16
    )


def body(record, chips, steer_lags):
    hyd_local = record.shape[1]
    tm_size = lax.axis_size("tm")
    local_periods = PERIODS // tm_size
    delay_rows = DELAYS // tm_size
    seg_len = CODE + DELAYS - 1
    norm_code = 1.0 / math.sqrt(CODE)
    tail_rows = passed_along(record[: DELAYS - 1], "tm", -1)
    extended = jnp.concatenate([record, tail_rows], 0)
    toeplitz = toeplitz_code(chips)
    profile_list = []
    for period in range(local_periods):
        segment = extended[period * CODE : period * CODE + seg_len]
        profile_list.append(
            (jnp.dot(toeplitz, segment, preferred_element_type=jnp.float32) * norm_code).astype(
                jnp.bfloat16
            )
        )
    profiles = jnp.stack(profile_list, 0)
    transform = dft_table(PERIODS)
    received = lax.all_to_all(profiles, "tm", split_axis=1, concat_axis=0, tiled=True)
    trailing = received.shape[1:]
    flattened = received.reshape(received.shape[0], -1)
    spectral = jnp.dot(transform, flattened, preferred_element_type=jnp.float32).astype(
        jnp.bfloat16
    )
    spectrum = spectral.reshape((2, received.shape[0]) + trailing)
    next_rows = passed_along(spectrum[:, :, : MAXLAG - 1, :], "tm", -1)
    spec_ext = jnp.concatenate([spectrum, next_rows], 2)
    norm_hydro = 1.0 / math.sqrt(HYDRO)
    shifted_list = [
        spec_ext[:, :, offset : offset + delay_rows, :].reshape(2 * PERIODS * delay_rows, hyd_local)
        for offset in range(MAXLAG)
    ]
    beam_local = BEAMS // lax.axis_size("hyd")
    partial_sum = jnp.zeros((2 * PERIODS * delay_rows, BEAMS), jnp.float32)
    for offset in range(MAXLAG):
        selector = (steer_lags == offset).astype(jnp.bfloat16)
        partial_sum = partial_sum + jnp.dot(
            shifted_list[offset], selector, preferred_element_type=jnp.float32
        )
    summed = lax.psum(partial_sum * norm_hydro, "hyd")
    owned = lax.dynamic_slice_in_dim(summed, lax.axis_index("hyd") * beam_local, beam_local, 1)
    owned = owned.reshape(2, PERIODS, delay_rows, beam_local)
    return owned[0] * owned[0] + owned[1] * owned[1]


def solution(mesh):
    in_specs = (P(("runs", "tm"), "hyd"), P(), P("hyd", None))
    out_specs = P("runs", "tm", "hyd")
    return jax.shard_map(body, mesh=mesh, in_specs=in_specs, out_specs=out_specs, check_vma=False)
```

profile of v0, /device:TPU:0, one launch (start us, length us, event | category | flops | bytes accessed | tf_op | source)
XLA Modules:
  0.0 408.6 jit_solution(9783359401931948476)
XLA Ops:
  6.5 1.1 slice.73
  7.6 1.3 collective-permute-start
  8.9 0.7 convert_element_type.49
  9.6 2.5 tile.10
  12.1 11.8 %tile.11 = bf16[2358784]{0:T(1024)(128)(2,1)} reshape(bf16[512,4607]{1,0:T(8,128)(2,1)} %tile.10) | data formatting | bytes 9435136 | tf_op jit(solution)/shard_map/tile | solution.py:24
  23.9 5.7 %slice.85 = bf16[2358272]{0:T(1024)(128)(2,1)} slice(bf16[2358784]{0:T(1024)(128)(2,1)} %tile.11), slice={[0:2358272]} | slice | bytes 9433088 | tf_op jit(solution)/shard_map/slice | solution.py:24
  29.6 11.3 %convert_element_type.50 = bf16[512,4606]{1,0:T(8,128)(2,1)} reshape(bf16[2358272]{0:T(1024)(128)(2,1)} %slice.85) | data formatting | bytes 9433088 | tf_op jit(solution)/shard_map/convert_element_type | solution.py:25
  40.9 7.3 %fusion.65 = bf16[8,512,512]{2,1,0:T(8,128)(2,1)} fusion(bf16[512,4606]{1,0:T(8,128)(2,1)} %convert_element_type.50, bf16[32760,512]{1,0:T(8,128)(2,1)} %param.3), kind=kOutput, calls=%fused_computation.47 | convolution fusion | flops 2415394816 | bytes 9961472 | tf_op jit(solution)/shard_map/dot_general | solution.py:51
  48.3 0.0 slice-start.5
  48.3 5.9 %fusion.73 = bf16[8,512,512]{2,1,0:T(8,128)(2,1)} fusion(bf16[8,512,512]{2,1,0:T(8,128)(2,1)} %fusion.65, bf16[512,4606]{1,0:T(8,128)(2,1)S(1)} %copy-done.1, bf16[32760,512]{1,0:T(8,128)(2,1)} %param.3), kind=kOutput, calls=%fused_computation.51 | convolution fusion | flops 2415394816 | bytes 9959424 | tf_op jit(solution)/shard_map/dot_general | solution.py:51
  54.2 6.6 %fusion.79 = bf16[8,512,512]{2,1,0:T(8,128)(2,1)} fusion(bf16[8,512,512]{2,1,0:T(8,128)(2,1)} %fusion.73, bf16[512,4606]{1,0:T(8,128)(2,1)S(1)} %copy-done.1, bf16[32760,512]{1,0:T(8,128)(2,1)} %param.3), kind=kOutput, calls=%fused_computation.53 | convolution fusion | flops 2415394816 | bytes 9959424 | tf_op jit(solution)/shard_map/dot_general | solution.py:51
  60.9 0.0 slice-done.8
  60.9 1.4 slice-done.9
  62.3 3.7 fusion.85
  66.0 3.5 fusion.91
  69.5 3.5 fusion.97
  73.0 3.5 fusion.103
  76.5 0.0 collective-permute-done
  76.5 5.9 %fusion.69 = bf16[8,512,512]{2,1,0:T(8,128)(2,1)} fusion(bf16[8,512,512]{2,1,0:T(8,128)(2,1)} %fusion.103, bf16[512,4606]{1,0:T(8,128)(2,1)} %convert_element_type.50, bf16[511,512]{1,0:T(8,128)(2,1)S(1)} %collective-permute-done, bf16[32760,512]{1,0:T(8,128)(2,1)S(1)} %bitcast.82), kind=kOutput, calls=%fused_computation.49 | convolution fusion | flops 2424827904 | bytes 39312384 | tf_op jit(solution)/shard_map/dot_general | solution.py:51
  82.5 6.9 %copy.5 = bf16[8,512,512]{2,0,1:T(8,128)(2,1)} copy(bf16[8,512,512]{2,1,0:T(8,128)(2,1)} %fusion.69) | data formatting | bytes 8388608 | tf_op jit(solution)/shard_map/stack | solution.py:55
  89.3 8.4 %all-to-all-start = ((bf16[8,512,512]{2,0,1:T(8,128)(2,1)}), bf16[8,512,512]{2,0,1:T(8,128)(2,1)}, u32[]{:S(2)}, u32[]{:S(2)}) async-start(bf16[8,512,512]{2,0,1:T(8,128)(2,1)} %copy.5), calls=%async_computation | async-start | bytes 8388608 | tf_op jit(solution)/shard_map/all_to_all | solution.py:57
  97.8 0.0 all-reduce.3.cloned.1.call-start
  97.8 0.2 multiply_convert_fusion
  98.0 92.8 %all-to-all-done = bf16[8,512,512]{2,0,1:T(8,128)(2,1)} async-done(((bf16[8,512,512]{2,0,1:T(8,128)(2,1)}), bf16[8,512,512]{2,0,1:T(8,128)(2,1)}, u32[]{:S(2)}, u32[]{:S(2)}) %all-to-all-start) | async-done | bytes 4194336 | tf_op jit(solution)/shard_map/all_to_all | solution.py:57
  190.8 3.8 copy.14
  194.6 2.6 copy.10
  197.1 5.6 %convolution_convert_fusion = bf16[128,32768]{1,0:T(8,128)(2,1)} fusion(bf16[64,32768]{1,0:T(8,128)(2,1)S(1)} %bitcast.83, bf16[64,64]{1,0:T(8,128)(2,1)S(1)} %get-tuple-element.12, bf16[64,64]{1,0:T(8,128)(2,1)S(1)} %get-tuple-element.13), kind=kOutput, calls=%fused_computation | convolution fusion | flops 541097984 | bytes 12599296 | tf_op jit(solution)/shard_map/dot_general | solution.py:60
  202.7 13.6 %reshape_reshape.3 = bf16[8192,512]{1,0:T(8,128)(2,1)} reshape(bf16[128,32768]{1,0:T(8,128)(2,1)} %convolution_convert_fusion) | data formatting | bytes 16777216 | tf_op jit(solution)/shard_map/reshape;reshape | solution.py:68
  216.3 10.2 %copy.11 = bf16[16,8,64,512]{3,2,1,0:T(8,128)(2,1)} copy(bf16[16,8,64,512]{3,1,2,0:T(8,128)(2,1)} %bitcast.69) | data formatting | bytes 16777216
  226.6 8.0 %constant_dynamic-update-slice_fusion = bf16[2,64,71,512]{3,2,1,0:T(8,128)(2,1)} fusion(bf16[2,64,64,512]{3,2,1,0:T(8,128)(2,1)} %bitcast.79), kind=kLoop, calls=%fused_computation.94 | loop fusion | bytes 16777216
  234.6 1.3 slice.86
  235.9 0.3 copy.9
  236.2 1.3 collective-permute-start.1
  237.5 9.1 %fusion.113 = f32[8192,256]{1,0:T(8,128)} fusion(bf16[8192,512]{1,0:T(8,128)(2,1)} %reshape_reshape.3, s32[512,256]{1,0:T(8,128)S(1)} %copy-done), kind=kOutput, calls=%fused_computation.70 | convolution fusion | flops 2147614720 | bytes 17301504 | tf_op jit(solution)/shard_map/dot_general | solution.py:75
  246.7 12.5 %collective-permute-done.1 = bf16[2,64,7,512]{3,1,2,0:T(8,128)(2,1)S(1)} collective-permute-done((bf16[2,64,7,512]{3,1,2,0:T(8,128)(2,1)S(1)}, bf16[2,64,7,512]{3,1,2,0:T(8,128)(2,1)S(1)}, u32[]{:S(2)}, u32[]{:S(2)}) %collective-permute-start.1) | collective-permute-done | bytes 917536 | tf_op jit(solution)/shard_map/ppermute | solution.py:18
  259.1 1.6 copy_dynamic-update-slice_fusion
  260.7 52.8 %fusion.142 = (bf16[2,64,64,512]{3,2,1,0:T(8,128)(2,1)}, bf16[2,64,64,512]{3,2,1,0:T(8,128)(2,1)}, bf16[2,64,64,512]{3,2,1,0:T(8,128)(2,1)}, bf16[2,64,64,512]{3...) fusion(bf16[2,64,71,512]{3,2,1,0:T(8,128)(2,1)} %copy_dynamic-u, ...), kind=kLoop, calls=%fused_computation.106 | loop fusion | bytes 117440512 | tf_op jit(solution)/shard_map/slice | solution.py:68
  313.6 8.4 %convolution_add_fusion.6 = f32[8192,256]{1,0:T(8,128)S(1)} fusion(f32[8192,256]{1,0:T(8,128)} %fusion.113, bf16[8192,512]{1,0:T(8,128)(2,1)} %bitcast.78, s32[512,256]{1,0:T(8,128)S(1)} %copy-done), kind=kOutput, calls=%fused_computation.8 | convolution fusion | flops 2149711872 | bytes 25690112 | tf_op jit(solution)/shard_map/dot_general | solution.py:75
  322.0 0.0 slice-start
  322.0 6.1 %convolution_add_fusion.5 = f32[8192,256]{1,0:T(8,128)S(1)} fusion(f32[8192,256]{1,0:T(8,128)S(1)} %convolution_add_fusion.6, bf16[8192,512]{1,0:T(8,128)(2,1)} %bitcast.77, s32[512,256]{1,0:T(8,128)S(1)} %copy-done), kind=kOutput, calls=%fused_computation.7 | convolution fusion | flops 2149711872 | bytes 25690112 | tf_op jit(solution)/shard_map/dot_general | solution.py:75
  328.1 6.1 %convolution_add_fusion.4 = f32[8192,256]{1,0:T(8,128)S(1)} fusion(f32[8192,256]{1,0:T(8,128)S(1)} %convolution_add_fusion.5, bf16[8192,512]{1,0:T(8,128)(2,1)} %bitcast.76, s32[512,256]{1,0:T(8,128)S(1)} %copy-done), kind=kOutput, calls=%fused_computation.6 | convolution fusion | flops 2149711872 | bytes 25690112 | tf_op jit(solution)/shard_map/dot_general | solution.py:75
  334.3 2.4 convolution_add_fusion.3
  336.7 6.3 %convolution_add_fusion.2 = f32[8192,256]{1,0:T(8,128)S(1)} fusion(f32[8192,256]{1,0:T(8,128)S(1)} %convolution_add_fusion.3, bf16[8192,512]{1,0:T(8,128)(2,1)} %bitcast.72, s32[512,256]{1,0:T(8,128)S(1)} %copy-done), kind=kOutput, calls=%fused_computation.4 | convolution fusion | flops 2149711872 | bytes 25690112 | tf_op jit(solution)/shard_map/dot_general | solution.py:75
  343.0 6.0 %convolution_add_fusion.1 = f32[8192,256]{1,0:T(8,128)S(1)} fusion(f32[8192,256]{1,0:T(8,128)S(1)} %convolution_add_fusion.2, bf16[8192,512]{1,0:T(8,128)(2,1)} %bitcast.71, s32[512,256]{1,0:T(8,128)S(1)} %copy-done), kind=kOutput, calls=%fused_computation.3 | convolution fusion | flops 2149711872 | bytes 25690112 | tf_op jit(solution)/shard_map/dot_general | solution.py:75
  349.0 9.2 %fusion = f32[8192,256]{1,0:T(8,128)} fusion(f32[8192,256]{1,0:T(8,128)S(1)} %convolution_add_fusion.1, bf16[8192,512]{1,0:T(8,128)(2,1)} %bitcast.70, s32[512,256]{1,0:T(8,128)S(1)} %copy-done), kind=kOutput, calls=%fused_computation.2 | convolution fusion | flops 2151809024 | bytes 25690112 | tf_op jit(solution)/shard_map/dot_general | solution.py:75
  358.2 0.0 all-reduce.3.cloned.1.call-update
  358.2 39.2 %all-reduce.3.cloned.1.call-done = f32[8192,256]{1,0:T(8,128)} async-done(((f32[8192,256]{1,0:T(8,128)}), f32[8192,256]{1,0:T(8,128)}) %all-reduce.3.cloned.1.call-update) | async-done | bytes 8388624 | tf_op jit(solution)/shard_map/psum | solution.py:78
  397.5 3.8 fusion.17
  (23 shorter events, 0.0 us)
Async XLA Ops:
  7.6 68.9 %collective-permute-start = (bf16[511,512]{1,0:T(8,128)(2,1)S(1)}, bf16[511,512]{1,0:T(8,128)(2,1)S(1)}, u32[]{:S(2)}, u32[]{:S(2)}) collective-permute-start(bf16[511,512]{1,0:T(8,128)(2,1)S(1)} %slice.73), channel_id=1, source_target_pairs={{2,0},{4,2},{6,4},{8,6},{10,8},{12,10},{14,12},{3,1},{5,3},{7,5},{... | collective-permute-start | bytes 1569800 | tf_op jit(solution)/shard_map/ppermute | solution.py:18
  40.9 7.3 %copy-start.1 = (bf16[512,4606]{1,0:T(8,128)(2,1)S(1)}, bf16[512,4606]{1,0:T(8,128)(2,1)}, u32[]{:S(2)}) copy-start(bf16[512,4606]{1,0:T(8,128)(2,1)} %convert_element_type.50) | copy-start | bytes 14149636
  48.2 12.6 %slice-start.2 = ((s8[33546240]{0:T(1024)(128)(4,1)}), s8[4194304]{0:T(1024)(128)(4,1)S(1)}, s32[]{:S(2)}) async-start(s8[33546240]{0:T(1024)(128)(4,1)} %bitcast.81), calls=%async_computation.4 | async-start | bytes 8388608
  48.2 12.6 %slice-start.3 = ((s8[33546240]{0:T(1024)(128)(4,1)}), s8[4194304]{0:T(1024)(128)(4,1)S(1)}, s32[]{:S(2)}) async-start(s8[33546240]{0:T(1024)(128)(4,1)} %bitcast.81), calls=%async_computation.5 | async-start | bytes 8388608
  48.2 12.6 %slice-start.4 = ((s8[33546240]{0:T(1024)(128)(4,1)}), s8[4194304]{0:T(1024)(128)(4,1)S(1)}, s32[]{:S(2)}) async-start(s8[33546240]{0:T(1024)(128)(4,1)} %bitcast.81), calls=%async_computation.6 | async-start | bytes 8388608
  48.3 12.6 %slice-start.5 = ((s8[33546240]{0:T(1024)(128)(4,1)}), s8[4194304]{0:T(1024)(128)(4,1)S(1)}, s32[]{:S(2)}) async-start(s8[33546240]{0:T(1024)(128)(4,1)} %bitcast.81), calls=%async_computation.7 | async-start | bytes 8388608
  48.3 12.6 %slice-start.6 = ((s8[33546240]{0:T(1024)(128)(4,1)}), s8[4194304]{0:T(1024)(128)(4,1)S(1)}, s32[]{:S(2)}) async-start(s8[33546240]{0:T(1024)(128)(4,1)} %bitcast.81), calls=%async_computation.8 | async-start | bytes 8388608
  54.2 6.6 %slice-start.7 = ((s8[33546240]{0:T(1024)(128)(4,1)}), s8[4194304]{0:T(1024)(128)(4,1)S(1)}, s32[]{:S(2)}) async-start(s8[33546240]{0:T(1024)(128)(4,1)} %bitcast.81), calls=%async_computation.9 | async-start | bytes 8388608
  54.2 6.7 %slice-start.8 = ((s8[33546240]{0:T(1024)(128)(4,1)}), s8[4194304]{0:T(1024)(128)(4,1)S(1)}, s32[]{:S(2)}) async-start(s8[33546240]{0:T(1024)(128)(4,1)} %bitcast.81), calls=%async_computation.10 | async-start | bytes 8388608
  54.2 8.0 %slice-start.9 = ((s8[33546240]{0:T(1024)(128)(4,1)}), s8[4186112]{0:T(1024)(128)(4,1)S(1)}, s32[]{:S(2)}) async-start(s8[33546240]{0:T(1024)(128)(4,1)} %bitcast.81), calls=%async_computation.11 | async-start | bytes 8372224
  89.3 101.4 %all-to-all-start = ((bf16[8,512,512]{2,0,1:T(8,128)(2,1)}), bf16[8,512,512]{2,0,1:T(8,128)(2,1)}, u32[]{:S(2)}, u32[]{:S(2)}) async-start(bf16[8,512,512]{2,0,1:T(8,128)(2,1)} %copy.5), calls=%async_computation | async-start | bytes 8388608 | tf_op jit(solution)/shard_map/all_to_all | solution.py:57
  97.8 299.7 %all-reduce.3.cloned.1.call-start = ((), (), s32[]{:S(2)}) async-start(), calls=%async_computation.1 | async-start | bytes 16777216 | tf_op jit(solution)/shard_map/psum | solution.py:78
  226.6 10.9 %copy-start = (s32[512,256]{1,0:T(8,128)S(1)}, s32[512,256]{1,0:T(8,128)}, u32[]{:S(2)}) copy-start(s32[512,256]{1,0:T(8,128)} %param.5) | copy-start | bytes 1572868
  236.2 22.9 %collective-permute-start.1 = (bf16[2,64,7,512]{3,1,2,0:T(8,128)(2,1)S(1)}, bf16[2,64,7,512]{3,1,2,0:T(8,128)(2,1)S(1)}, u32[]{:S(2)}, u32[]{:S(2)}) collective-permute-start(bf16[2,64,7,512]{3,1,2,0:T(8,128)(2,1)S(1)} %copy.9), channel_id=1, source_target_pairs={{2,0},{4,2},{6,4},{8,6},{10,8},{12,10},{14,12},{3,1},{5,3},{7,5},{... | collective-permute-start | bytes 2752520 | tf_op jit(solution)/shard_map/ppermute | solution.py:18
  322.0 12.3 %slice-start = ((s8[8388608]{0:T(1024)(128)(4,1)}), s8[4194304]{0:T(1024)(128)(4,1)S(1)}, s32[]{:S(2)}) async-start(s8[8388608]{0:T(1024)(128)(4,1)} %bitcast.73), calls=%async_computation.2 | async-start | bytes 8388608
  328.1 6.2 %slice-start.1 = ((s8[8388608]{0:T(1024)(128)(4,1)}), s8[4194304]{0:T(1024)(128)(4,1)S(1)}, s32[]{:S(2)}) async-start(s8[8388608]{0:T(1024)(128)(4,1)} %bitcast.73), calls=%async_computation.3 | async-start | bytes 8388608
Sparse Core Ops, SparseCore 0:
  358.3 39.0 all-reduce.2
where the time goes:
time: 416 us; the launch traced here: 409 us
  waiting for transfers between devices  145 us (35%)
  local copies, waits for them, and re-layouts  135 us (32%)
  matrix products  99.3 us (24%)
  between operations  14.1 us (3%)
  starting transfers between devices  11 us (3%)
  other arithmetic  4.64 us (1%)
    all_to_all x1, waiting for transfers between devices, body(): lax.all_to_all(profiles, 'tm', split_axis=1, concat_axis=0, tiled=True)  92.8 us
    dot_general x8, matrix products, body(): jnp.dot(shifted_list[offset], selector, preferred_element_type=jnp.float32)  53.7 us
    slice x1, local copies, waits for them, and re-layouts, body(): spec_ext[:, :, offset:offset + delay_rows, :]  52.8 us
    dot_general x8, matrix products, body(): jnp.dot(toeplitz, segment, preferred_element_type=jnp.float32) * norm_code  40 us
    psum x1, waiting for transfers between devices, body(): summed = lax.psum(partial_sum * norm_hydro, 'hyd')  39.2 us
    unnamed x28, local copies, waits for them, and re-layouts  22.6 us
    another operation x2, local copies, waits for them, and re-layouts, toeplitz_code(): tiled = jnp.tile(padded, DELAYS)[:DELAYS * seg_len]  14.3 us
    another operation x1, local copies, waits for them, and re-layouts, body(): spec_ext[:, :, offset:offset + delay_rows, :]  13.6 us
  transfers between devices with their start and end apart: 4, of which 3 were waited for; matrix products, arithmetic and copies ran while one was open for 18% of the time, Pallas kernels for 0%

commit v1 on v0

--- a/solution.py
+++ b/solution.py
@@ -10,6 +10,22 @@
 PERIODS = 64
 BEAMS = 256
 MAXLAG = 8
+
+
+def zone_fit(chunk, dimension_no, xx):
+    main = chunk.shape
+    even = chunk.reshape(
+        *main[:dimension_no], xx, main[dimension_no] // xx, *main[dimension_no + 1 :]
+    )
+    z1 = jnp.moveaxis(even, dimension_no, 0)
+    return z1
+
+
+def measure_stacks_all_all(base_x, ndim_at):
+    item_now = list(base_x.shape[1:])
+    item_now[ndim_at] *= base_x.shape[0]
+    part_next = jnp.moveaxis(base_x, 0, ndim_at).reshape(item_now)
+    return part_next
 
 
 def passed_along(array, axis, by):
@@ -54,7 +70,18 @@
         )
     profiles = jnp.stack(profile_list, 0)
     transform = dft_table(PERIODS)
-    received = lax.all_to_all(profiles, "tm", split_axis=1, concat_axis=0, tiled=True)
+    latest, reply = (lax.axis_size("tm"), lax.axis_index("tm"))
+    y2 = zone_fit(profiles, 1, latest)
+    u1 = y2
+    for pp in range(1, latest):
+        newest, seen_now = ((reply + pp) % latest, (reply - pp) % latest)
+        val = lax.dynamic_index_in_dim(y2, newest, 0)
+        chunks = []
+        for ix in range(latest):
+            chunks.append((ix, (ix + pp) % latest))
+        a_now = lax.ppermute(val, "tm", chunks)
+        u1 = lax.dynamic_update_slice_in_dim(u1, a_now, seen_now, axis=0)
+    received = measure_stacks_all_all(u1, 0)
     trailing = received.shape[1:]
     flattened = received.reshape(received.shape[0], -1)
     spectral = jnp.dot(transform, flattened, preferred_element_type=jnp.float32).astype(

time: 416 us -> 421 us (1.012)
  waiting for transfers between devices: 145 us -> 117 us
  local copies, waits for them, and re-layouts: 135 us -> 154 us
  starting transfers between devices: 11 us -> 26.3 us
    all_to_all x1 -> x0, waiting for transfers between devices: 92.8 us -> none  [body(): lax.all_to_all(profiles, 'tm', split_axis=1, concat_axis=0, tiled=True)]
    ppermute x0 -> x7, waiting for transfers between devices: none -> 38.6 us  [body(): a_now = lax.ppermute(val, 'tm', chunks)]
    ppermute x0 -> x7, starting transfers between devices: none -> 23.3 us  [body(): a_now = lax.ppermute(val, 'tm', chunks)]
    psum x1, waiting for transfers between devices: 39.2 us -> 58.6 us  [body(): summed = lax.psum(partial_sum * norm_hydro, 'hyd')]
    unnamed x28 -> x35, local copies, waits for them, and re-layouts: 22.6 us -> 37 us
    dynamic_update_slice x0 -> x7, local copies, waits for them, and re-layouts: none -> 11.2 us  [body(): u1 = lax.dynamic_update_slice_in_dim(u1, a_now, seen_now, axis=0)]
    all_to_all x1 -> x0, starting transfers between devices: 8.43 us -> none  [body(): lax.all_to_all(profiles, 'tm', split_axis=1, concat_axis=0, tiled=True)]
    ppermute x2, waiting for transfers between devices: 12.5 us -> 19.6 us  [passed_along(): return lax.ppermute(array, axis, pairs)]
  transfers between devices with their start and end apart: 4 -> 10, of which waited for: 3 -> 5; matrix products, arithmetic and copies ran while one was open for 18% -> 23% of each run, Pallas kernels for 0% -> 0%
where the time goes in v1:
time: 421 us; the launch traced here: 414 us
  local copies, waits for them, and re-layouts  154 us (37%)
  waiting for transfers between devices  117 us (28%)
  matrix products  98.3 us (23%)
  starting transfers between devices  26.3 us (6%)
  between operations  14 us (3%)
  other arithmetic  4.63 us (1%)
    psum x1, waiting for transfers between devices, body(): summed = lax.psum(partial_sum * norm_hydro, 'hyd')  58.6 us
    dot_general x8, matrix products, body(): jnp.dot(shifted_list[offset], selector, preferred_element_type=jnp.float32)  53.6 us
    slice x1, local copies, waits for them, and re-layouts, body(): spec_ext[:, :, offset:offset + delay_rows, :]  52.8 us
    dot_general x8, matrix products, body(): jnp.dot(toeplitz, segment, preferred_element_type=jnp.float32) * norm_code  39.1 us
    ppermute x7, waiting for transfers between devices, body(): a_now = lax.ppermute(val, 'tm', chunks)  38.6 us
    unnamed x35, local copies, waits for them, and re-layouts  37 us
    ppermute x7, starting transfers between devices, body(): a_now = lax.ppermute(val, 'tm', chunks)  23.3 us
    ppermute x2, waiting for transfers between devices, passed_along(): return lax.ppermute(array, axis, pairs)  19.6 us
  transfers between devices with their start and end apart: 10, of which 5 were waited for; matrix products, arithmetic and copies ran while one was open for 23% of the time, Pallas kernels for 0%

profile of v1, /device:TPU:0, one launch (start us, length us, event | category | flops | bytes accessed | tf_op | source)
XLA Modules:
  0.0 413.8 jit_solution(959727972618772256)
XLA Ops:
  9.6 2.5 tile.10
  12.2 11.8 %tile.11 = bf16[2358784]{0:T(1024)(128)(2,1)} reshape(bf16[512,4607]{1,0:T(8,128)(2,1)} %tile.10) | data formatting | bytes 9435136 | tf_op jit(solution)/shard_map/tile | solution.py:40
  23.9 5.9 %slice.85 = bf16[2358272]{0:T(1024)(128)(2,1)} slice(bf16[2358784]{0:T(1024)(128)(2,1)} %tile.11), slice={[0:2358272]} | slice | bytes 9433088 | tf_op jit(solution)/shard_map/slice | solution.py:40
  29.9 11.3 %convert_element_type.50 = bf16[512,4606]{1,0:T(8,128)(2,1)} reshape(bf16[2358272]{0:T(1024)(128)(2,1)} %slice.85) | data formatting | bytes 9433088 | tf_op jit(solution)/shard_map/convert_element_type | solution.py:41
  41.2 7.3 %fusion.59 = bf16[512,512]{1,0:T(8,128)(2,1)} fusion(bf16[512,4606]{1,0:T(8,128)(2,1)} %convert_element_type.50, bf16[32760,512]{1,0:T(8,128)(2,1)} %param.3), kind=kOutput, calls=%fused_computation.44 | convolution fusion | flops 2415394816 | bytes 9961472 | tf_op jit(solution)/shard_map/dot_general | solution.py:67
  48.5 5.9 %fusion.55 = bf16[512,512]{1,0:T(8,128)(2,1)} fusion(bf16[512,4606]{1,0:T(8,128)(2,1)S(1)} %copy-done.1, bf16[32760,512]{1,0:T(8,128)(2,1)} %param.3), kind=kOutput, calls=%fused_computation.42 | convolution fusion | flops 2415394816 | bytes 9959424 | tf_op jit(solution)/shard_map/dot_general | solution.py:67
  54.5 6.6 %fusion.52 = bf16[512,512]{1,0:T(8,128)(2,1)} fusion(bf16[512,4606]{1,0:T(8,128)(2,1)S(1)} %copy-done.1, bf16[32760,512]{1,0:T(8,128)(2,1)} %param.3), kind=kOutput, calls=%fused_computation.41 | convolution fusion | flops 2415394816 | bytes 9959424 | tf_op jit(solution)/shard_map/dot_general | solution.py:67
  62.5 3.6 fusion.49
  66.2 3.4 fusion.46
  69.6 3.4 fusion.43
  73.0 2.6 fusion.40
  75.6 1.9 constant_dynamic-update-slice_fusion.7
  77.5 1.9 constant_dynamic-update-slice_fusion.6
  79.4 1.9 constant_dynamic-update-slice_fusion.5
  81.3 1.9 constant_dynamic-update-slice_fusion.4
  83.2 1.9 constant_dynamic-update-slice_fusion.3
  85.1 1.9 constant_dynamic-update-slice_fusion.2
  87.9 6.3 %fusion.58 = bf16[512,512]{1,0:T(8,128)(2,1)S(1)} fusion(bf16[512,4606]{1,0:T(8,128)(2,1)} %convert_element_type.50, bf16[511,512]{1,0:T(8,128)(2,1)S(1)} %collective-permute-done, bf16[32760,512]{1,0:T(8,128)(2,1)} %param.3), kind=kOutput, calls=%fused_computation.43 | convolution fusion | flops 2424827904 | bytes 39310336 | tf_op jit(solution)/shard_map/dot_general | solution.py:67
  95.0 3.1 dynamic-slice_bitcast_fusion
  98.1 3.6 collective-permute-start.1
  101.7 2.1 collective-permute-start.2
  103.8 3.6 collective-permute-start.3
  110.7 7.9 %collective-permute-done.1 = bf16[1,8,64,512]{3,2,1,0:T(8,128)(2,1)} collective-permute-done((bf16[1,8,64,512]{3,2,1,0:T(8,128)(2,1)}, bf16[1,8,64,512]{3,2,1,0:T(8,128)(2,1)}, u32[]{:S(2)}, u32[]{:S(2)}) %collective-permute-start.1) | collective-permute-done | bytes 524320 | tf_op jit(solution)/shard_map/ppermute | solution.py:82
  118.6 2.7 collective-permute-start.6
  121.3 1.9 constant_dynamic-update-slice_fusion.15
  123.2 8.3 %collective-permute-start.7 = (bf16[1,8,64,512]{3,2,1,0:T(8,128)(2,1)S(1)}, bf16[1,8,64,512]{3,2,1,0:T(8,128)(2,1)S(1)}, u32[]{:S(2)}, u32[]{:S(2)}) collective-permute-start(bf16[1,8,64,512]{3,2,1,0:T(8,128)(2,1)S(1)} %get-tuple-element.12), channel_id=1, source_target_pairs={{0,14},{2,0},{4,2},{6,4},{8,6},{10,8},{12,10},{14,12},{1,15},{3,1}... | collective-permute-start | bytes 1572872 | tf_op jit(solution)/shard_map/ppermute | solution.py:82
  131.5 1.9 constant_dynamic-update-slice_fusion.14
  133.5 28.9 %collective-permute-done.3 = bf16[1,8,64,512]{3,2,1,0:T(8,128)(2,1)} collective-permute-done((bf16[1,8,64,512]{3,2,1,0:T(8,128)(2,1)S(1)}, bf16[1,8,64,512]{3,2,1,0:T(8,128)(2,1)}, u32[]{:S(2)}, u32[]{:S(2)}) %collective-permute-start.3) | collective-permute-done | bytes 524320 | tf_op jit(solution)/shard_map/ppermute | solution.py:82
  162.3 1.9 constant_dynamic-update-slice_fusion.13
  164.2 1.9 constant_dynamic-update-slice_fusion.12
  166.1 1.9 constant_dynamic-update-slice_fusion.11
  171.5 4.7 %copy.23 = bf16[8,8,64,512]{3,1,2,0:T(8,128)(2,1)S(1)} copy(bf16[8,8,64,512]{3,2,1,0:T(8,128)(2,1)} %constant_dynamic-update-slice_fusion.9) | data formatting | bytes 8388608
  176.2 5.6 %convolution_convert_fusion = bf16[128,32768]{1,0:T(8,128)(2,1)} fusion(bf16[64,32768]{1,0:T(8,128)(2,1)S(1)} %bitcast.86, bf16[64,64]{1,0:T(8,128)(2,1)S(1)} %get-tuple-element.19, bf16[64,64]{1,0:T(8,128)(2,1)S(1)} %get-tuple-element.20), kind=kOutput, calls=%fused_computation | convolution fusion | flops 541097984 | bytes 12599296 | tf_op jit(solution)/shard_map/dot_general | solution.py:87
  181.8 13.5 %reshape_reshape.7 = bf16[8192,512]{1,0:T(8,128)(2,1)} reshape(bf16[128,32768]{1,0:T(8,128)(2,1)} %convolution_convert_fusion) | data formatting | bytes 16777216 | tf_op jit(solution)/shard_map/reshape;reshape | solution.py:95
  195.3 10.3 %copy.24 = bf16[16,8,64,512]{3,2,1,0:T(8,128)(2,1)} copy(bf16[16,8,64,512]{3,1,2,0:T(8,128)(2,1)} %bitcast.72) | data formatting | bytes 16777216
  205.5 7.9 %constant_dynamic-update-slice_fusion.8 = bf16[2,64,71,512]{3,2,1,0:T(8,128)(2,1)} fusion(bf16[2,64,64,512]{3,2,1,0:T(8,128)(2,1)} %bitcast.82), kind=kLoop, calls=%fused_computation.92 | loop fusion | bytes 16777216
  216.8 9.1 %fusion.69 = f32[8192,256]{1,0:T(8,128)} fusion(bf16[8192,512]{1,0:T(8,128)(2,1)} %reshape_reshape.7, s32[512,256]{1,0:T(8,128)S(1)} %copy-done), kind=kOutput, calls=%fused_computation.60 | convolution fusion | flops 2147614720 | bytes 17301504 | tf_op jit(solution)/shard_map/dot_general | solution.py:102
  225.9 19.6 %collective-permute-done.8 = bf16[2,64,7,512]{3,1,2,0:T(8,128)(2,1)S(1)} collective-permute-done((bf16[2,64,7,512]{3,1,2,0:T(8,128)(2,1)S(1)}, bf16[2,64,7,512]{3,1,2,0:T(8,128)(2,1)S(1)}, u32[]{:S(2)}, u32[]{:S(2)}) %collective-permute-start.8) | collective-permute-done | bytes 917536 | tf_op jit(solution)/shard_map/ppermute | solution.py:34
  247.0 52.8 %fusion.98 = (bf16[2,64,64,512]{3,2,1,0:T(8,128)(2,1)}, bf16[2,64,64,512]{3,2,1,0:T(8,128)(2,1)}, bf16[2,64,64,512]{3,2,1,0:T(8,128)(2,1)}, bf16[2,64,64,512]{3,...) fusion(bf16[2,64,71,512]{3,2,1,0:T(8,128)(2,1)} %copy_dynamic-u, ...), kind=kLoop, calls=%fused_computation.111 | loop fusion | bytes 117440512 | tf_op jit(solution)/shard_map/slice | solution.py:95
  299.8 8.4 %convolution_add_fusion.6 = f32[8192,256]{1,0:T(8,128)S(1)} fusion(f32[8192,256]{1,0:T(8,128)} %fusion.69, bf16[8192,512]{1,0:T(8,128)(2,1)} %bitcast.81, s32[512,256]{1,0:T(8,128)S(1)} %copy-done), kind=kOutput, calls=%fused_computation.8 | convolution fusion | flops 2149711872 | bytes 25690112 | tf_op jit(solution)/shard_map/dot_general | solution.py:102
  308.2 6.1 %convolution_add_fusion.5 = f32[8192,256]{1,0:T(8,128)S(1)} fusion(f32[8192,256]{1,0:T(8,128)S(1)} %convolution_add_fusion.6, bf16[8192,512]{1,0:T(8,128)(2,1)} %bitcast.80, s32[512,256]{1,0:T(8,128)S(1)} %copy-done), kind=kOutput, calls=%fused_computation.7 | convolution fusion | flops 2149711872 | bytes 25690112 | tf_op jit(solution)/shard_map/dot_general | solution.py:102
  314.4 6.1 %convolution_add_fusion.4 = f32[8192,256]{1,0:T(8,128)S(1)} fusion(f32[8192,256]{1,0:T(8,128)S(1)} %convolution_add_fusion.5, bf16[8192,512]{1,0:T(8,128)(2,1)} %bitcast.79, s32[512,256]{1,0:T(8,128)S(1)} %copy-done), kind=kOutput, calls=%fused_computation.6 | convolution fusion | flops 2149711872 | bytes 25690112 | tf_op jit(solution)/shard_map/dot_general | solution.py:102
  320.6 2.4 convolution_add_fusion.3
  323.0 6.2 %convolution_add_fusion.2 = f32[8192,256]{1,0:T(8,128)S(1)} fusion(f32[8192,256]{1,0:T(8,128)S(1)} %convolution_add_fusion.3, bf16[8192,512]{1,0:T(8,128)(2,1)} %bitcast.75, s32[512,256]{1,0:T(8,128)S(1)} %copy-done), kind=kOutput, calls=%fused_computation.4 | convolution fusion | flops 2149711872 | bytes 25690112 | tf_op jit(solution)/shard_map/dot_general | solution.py:102
  329.2 6.0 %convolution_add_fusion.1 = f32[8192,256]{1,0:T(8,128)S(1)} fusion(f32[8192,256]{1,0:T(8,128)S(1)} %convolution_add_fusion.2, bf16[8192,512]{1,0:T(8,128)(2,1)} %bitcast.74, s32[512,256]{1,0:T(8,128)S(1)} %copy-done), kind=kOutput, calls=%fused_computation.3 | convolution fusion | flops 2149711872 | bytes 25690112 | tf_op jit(solution)/shard_map/dot_general | solution.py:102
  335.2 9.1 %fusion = f32[8192,256]{1,0:T(8,128)} fusion(f32[8192,256]{1,0:T(8,128)S(1)} %convolution_add_fusion.1, bf16[8192,512]{1,0:T(8,128)(2,1)} %bitcast.73, s32[512,256]{1,0:T(8,128)S(1)} %copy-done), kind=kOutput, calls=%fused_computation.2 | convolution fusion | flops 2151809024 | bytes 25690112 | tf_op jit(solution)/shard_map/dot_general | solution.py:102
  344.4 58.6 %all-reduce.3.cloned.1.call-done = f32[8192,256]{1,0:T(8,128)} async-done(((f32[8192,256]{1,0:T(8,128)}), f32[8192,256]{1,0:T(8,128)}) %all-reduce.3.cloned.1.call-update) | async-done | bytes 8388624 | tf_op jit(solution)/shard_map/psum | solution.py:105
  402.9 3.8 fusion.17
  (49 shorter events, 17.8 us)
Async XLA Ops:
  6.5 396.4 %all-reduce.3.cloned.1.call-start = ((), (), s32[]{:S(2)}) async-start(), calls=%async_computation | async-start | bytes 16777216 | tf_op jit(solution)/shard_map/psum | solution.py:105
  7.6 80.3 %collective-permute-start = (bf16[511,512]{1,0:T(8,128)(2,1)S(1)}, bf16[511,512]{1,0:T(8,128)(2,1)S(1)}, u32[]{:S(2)}, u32[]{:S(2)}) collective-permute-start(bf16[511,512]{1,0:T(8,128)(2,1)S(1)} %slice.73), channel_id=1, source_target_pairs={{2,0},{4,2},{6,4},{8,6},{10,8},{12,10},{14,12},{3,1},{5,3},{7,5},{... | collective-permute-start | bytes 1569800 | tf_op jit(solution)/shard_map/ppermute | solution.py:34
  41.2 7.3 %copy-start.1 = (bf16[512,4606]{1,0:T(8,128)(2,1)S(1)}, bf16[512,4606]{1,0:T(8,128)(2,1)}, u32[]{:S(2)}) copy-start(bf16[512,4606]{1,0:T(8,128)(2,1)} %convert_element_type.50) | copy-start | bytes 14149636
  48.5 12.6 %slice-start.2 = ((s8[33546240]{0:T(1024)(128)(4,1)}), s8[4194304]{0:T(1024)(128)(4,1)S(1)}, s32[]{:S(2)}) async-start(s8[33546240]{0:T(1024)(128)(4,1)} %bitcast.84), calls=%async_computation.3 | async-start | bytes 8388608
  48.5 12.6 %slice-start.3 = ((s8[33546240]{0:T(1024)(128)(4,1)}), s8[4194304]{0:T(1024)(128)(4,1)S(1)}, s32[]{:S(2)}) async-start(s8[33546240]{0:T(1024)(128)(4,1)} %bitcast.84), calls=%async_computation.4 | async-start | bytes 8388608
  48.5 12.6 %slice-start.4 = ((s8[33546240]{0:T(1024)(128)(4,1)}), s8[4194304]{0:T(1024)(128)(4,1)S(1)}, s32[]{:S(2)}) async-start(s8[33546240]{0:T(1024)(128)(4,1)} %bitcast.84), calls=%async_computation.5 | async-start | bytes 8388608
  48.5 12.6 %slice-start.5 = ((s8[33546240]{0:T(1024)(128)(4,1)}), s8[4194304]{0:T(1024)(128)(4,1)S(1)}, s32[]{:S(2)}) async-start(s8[33546240]{0:T(1024)(128)(4,1)} %bitcast.84), calls=%async_computation.6 | async-start | bytes 8388608
  48.5 12.6 %slice-start.6 = ((s8[33546240]{0:T(1024)(128)(4,1)}), s8[4194304]{0:T(1024)(128)(4,1)S(1)}, s32[]{:S(2)}) async-start(s8[33546240]{0:T(1024)(128)(4,1)} %bitcast.84), calls=%async_computation.7 | async-start | bytes 8388608
  54.5 6.6 %slice-start.7 = ((s8[33546240]{0:T(1024)(128)(4,1)}), s8[4194304]{0:T(1024)(128)(4,1)S(1)}, s32[]{:S(2)}) async-start(s8[33546240]{0:T(1024)(128)(4,1)} %bitcast.84), calls=%async_computation.8 | async-start | bytes 8388608
  54.5 6.7 %slice-start.8 = ((s8[33546240]{0:T(1024)(128)(4,1)}), s8[4194304]{0:T(1024)(128)(4,1)S(1)}, s32[]{:S(2)}) async-start(s8[33546240]{0:T(1024)(128)(4,1)} %bitcast.84), calls=%async_computation.9 | async-start | bytes 8388608
  54.5 8.1 %slice-start.9 = ((s8[33546240]{0:T(1024)(128)(4,1)}), s8[4186112]{0:T(1024)(128)(4,1)S(1)}, s32[]{:S(2)}) async-start(s8[33546240]{0:T(1024)(128)(4,1)} %bitcast.84), calls=%async_computation.10 | async-start | bytes 8372224
  98.1 20.4 %collective-permute-start.1 = (bf16[1,8,64,512]{3,2,1,0:T(8,128)(2,1)}, bf16[1,8,64,512]{3,2,1,0:T(8,128)(2,1)}, u32[]{:S(2)}, u32[]{:S(2)}) collective-permute-start(bf16[1,8,64,512]{3,2,1,0:T(8,128)(2,1)} %get-tuple-element.18), channel_id=1, source_target_pairs={{0,2},{2,4},{4,6},{6,8},{8,10},{10,12},{12,14},{14,0},{1,3},{3,5},... | collective-permute-start | bytes 1572872 | tf_op jit(solution)/shard_map/ppermute | solution.py:82
  101.7 21.5 %collective-permute-start.2 = (bf16[1,8,64,512]{3,2,1,0:T(8,128)(2,1)S(1)}, bf16[1,8,64,512]{3,2,1,0:T(8,128)(2,1)}, u32[]{:S(2)}, u32[]{:S(2)}) collective-permute-start(bf16[1,8,64,512]{3,2,1,0:T(8,128)(2,1)S(1)} %get-tuple-element.17), channel_id=1, source_target_pairs={{0,4},{2,6},{4,8},{6,10},{8,12},{10,14},{12,0},{14,2},{1,5},{3,7},... | collective-permute-start | bytes 1572872 | tf_op jit(solution)/shard_map/ppermute | solution.py:82
  103.8 58.5 %collective-permute-start.3 = (bf16[1,8,64,512]{3,2,1,0:T(8,128)(2,1)S(1)}, bf16[1,8,64,512]{3,2,1,0:T(8,128)(2,1)}, u32[]{:S(2)}, u32[]{:S(2)}) collective-permute-start(bf16[1,8,64,512]{3,2,1,0:T(8,128)(2,1)S(1)} %get-tuple-element.16), channel_id=1, source_target_pairs={{0,6},{2,8},{4,10},{6,12},{8,14},{10,0},{12,2},{14,4},{1,7},{3,9},... | collective-permute-start | bytes 1572872 | tf_op jit(solution)/shard_map/ppermute | solution.py:82
  107.4 56.8 %collective-permute-start.4 = (bf16[1,8,64,512]{3,2,1,0:T(8,128)(2,1)S(1)}, bf16[1,8,64,512]{3,2,1,0:T(8,128)(2,1)}, u32[]{:S(2)}, u32[]{:S(2)}) collective-permute-start(bf16[1,8,64,512]{3,2,1,0:T(8,128)(2,1)S(1)} %get-tuple-element.15), channel_id=1, source_target_pairs={{0,8},{2,10},{4,12},{6,14},{8,0},{10,2},{12,4},{14,6},{1,9},{3,11}... | collective-permute-start | bytes 1572872 | tf_op jit(solution)/shard_map/ppermute | solution.py:82
  108.7 57.4 %collective-permute-start.5 = (bf16[1,8,64,512]{3,2,1,0:T(8,128)(2,1)S(1)}, bf16[1,8,64,512]{3,2,1,0:T(8,128)(2,1)}, u32[]{:S(2)}, u32[]{:S(2)}) collective-permute-start(bf16[1,8,64,512]{3,2,1,0:T(8,128)(2,1)S(1)} %get-tuple-element.14), channel_id=1, source_target_pairs={{0,10},{2,12},{4,14},{6,0},{8,2},{10,4},{12,6},{14,8},{1,11},{3,13... | collective-permute-start | bytes 1572872 | tf_op jit(solution)/shard_map/ppermute | solution.py:82
  118.6 49.4 %collective-permute-start.6 = (bf16[1,8,64,512]{3,2,1,0:T(8,128)(2,1)S(1)}, bf16[1,8,64,512]{3,2,1,0:T(8,128)(2,1)S(1)}, u32[]{:S(2)}, u32[]{:S(2)}) collective-permute-start(bf16[1,8,64,512]{3,2,1,0:T(8,128)(2,1)S(1)} %get-tuple-element.13), channel_id=1, source_target_pairs={{0,12},{2,14},{4,0},{6,2},{8,4},{10,6},{12,8},{14,10},{1,13},{3,15... | collective-permute-start | bytes 1572872 | tf_op jit(solution)/shard_map/ppermute | solution.py:82
  123.2 47.4 %collective-permute-start.7 = (bf16[1,8,64,512]{3,2,1,0:T(8,128)(2,1)S(1)}, bf16[1,8,64,512]{3,2,1,0:T(8,128)(2,1)S(1)}, u32[]{:S(2)}, u32[]{:S(2)}) collective-permute-start(bf16[1,8,64,512]{3,2,1,0:T(8,128)(2,1)S(1)} %get-tuple-element.12), channel_id=1, source_target_pairs={{0,14},{2,0},{4,2},{6,4},{8,6},{10,8},{12,10},{14,12},{1,15},{3,1}... | collective-permute-start | bytes 1572872 | tf_op jit(solution)/shard_map/ppermute | solution.py:82
  205.5 11.2 %copy-start = (s32[512,256]{1,0:T(8,128)S(1)}, s32[512,256]{1,0:T(8,128)}, u32[]{:S(2)}) copy-start(s32[512,256]{1,0:T(8,128)} %param.5) | copy-start | bytes 1572868
  215.1 30.4 %collective-permute-start.8 = (bf16[2,64,7,512]{3,1,2,0:T(8,128)(2,1)S(1)}, bf16[2,64,7,512]{3,1,2,0:T(8,128)(2,1)S(1)}, u32[]{:S(2)}, u32[]{:S(2)}) collective-permute-start(bf16[2,64,7,512]{3,1,2,0:T(8,128)(2,1)S(1)} %copy.22), channel_id=1, source_target_pairs={{2,0},{4,2},{6,4},{8,6},{10,8},{12,10},{14,12},{3,1},{5,3},{7,5},{... | collective-permute-start | bytes 2752520 | tf_op jit(solution)/shard_map/ppermute | solution.py:34
  308.2 12.3 %slice-start = ((s8[8388608]{0:T(1024)(128)(4,1)}), s8[4194304]{0:T(1024)(128)(4,1)S(1)}, s32[]{:S(2)}) async-start(s8[8388608]{0:T(1024)(128)(4,1)} %bitcast.76), calls=%async_computation.1 | async-start | bytes 8388608
  314.4 6.2 %slice-start.1 = ((s8[8388608]{0:T(1024)(128)(4,1)}), s8[4194304]{0:T(1024)(128)(4,1)S(1)}, s32[]{:S(2)}) async-start(s8[8388608]{0:T(1024)(128)(4,1)} %bitcast.76), calls=%async_computation.2 | async-start | bytes 8388608
Sparse Core Ops, SparseCore 0:
  344.5 58.4 all-reduce.2
